TPU v7x, 32 devices: a whole 2x2x4 slice. The times are simulated.
32 devices in a mesh: sensor: 16 (over z, y, core), day: 2 (over x).
Axes of the slice: x: 2, y: 2, z: 4, core: 2. Of those that a mesh axis runs over, the one named last changes fastest.
Arguments:
- y_obs: bfloat16 [2880, 2048], P('day', 'sensor'), may hold values from -256 to 256
- observed: int32 [2880, 2048], P('day', 'sensor'), may hold values 0 or 1
- day_factor: bfloat16 [10, 64], P('day'), may hold values from -6 to 6
- slot_factor: bfloat16 [288, 64], P('day'), may hold values from -6 to 6
- sensor_factor: bfloat16 [64, 2048], P(None, 'sensor'), may hold values from -6 to 6
- prior_scale: float32 [64], replicated, may hold values from 0.5 to 2
- neighbours: int32 [6, 2048], P(None, 'sensor'), may hold values from 0 to 2047, as said below
- edge_weight: float32 [6, 2048], P(None, 'sensor'), may hold values from 0.2 to 1
- noise: float32 [64, 2048], P(None, 'sensor'), may hold values from -6 to 6
Outputs:
- fresh_factor: float32 [64, 2048], P(None, 'sensor')
Inputs may be any that keep to these rules, and one draw needn't show every extreme that they name: Each sensor's neighbours are other sensors within 256 of it in index; its first two lie exactly that far away.
All inputs are finite; a program needn't handle non-finite values. No bound on the sum of `observed` on one device may be relied on, other than what follows from the above.
Results may differ from a plain program's by a relative error of at most 0.0023.
Values may be sent and summed in bfloat16 or wider, within the bound.
A program may use at most 64 MiB of HBM per device.

v0:
```python
import jax
import jax.numpy as jnp
from jax import lax
from jax.sharding import PartitionSpec as P


def shifted(shard, axis, by):
    size = lax.axis_size(axis)
    pairs = [(i, i + by) for i in range(size) if 0 <= i + by < size]
    return lax.ppermute(shard, axis, pairs)


def solve_block(gram_sums, right_sums, pulled, prior_diag, prior_scale, noise_rows, tau):
    count = gram_sums.shape[0]
    rank = right_sums.shape[1]
    squares = gram_sums.reshape(count, rank, rank)
    precision = tau * squares + prior_diag[:, None, None] * jnp.diag(prior_scale)[None, :, :]
    target = tau * right_sums + prior_scale[None, :] * pulled
    factor_low = jnp.linalg.cholesky(precision)
    halfway = lax.linalg.triangular_solve(
        factor_low, target[:, :, None], left_side=True, lower=True
    )
    centre_part = lax.linalg.triangular_solve(
        factor_low, halfway, left_side=True, lower=True, transpose_a=True
    )
    spread_part = lax.linalg.triangular_solve(
        factor_low, noise_rows[:, :, None], left_side=True, lower=True, transpose_a=True
    )
    return (centre_part + spread_part)[:, :, 0]


def shards(
    y_obs,
    observed,
    day_factor,
    slot_factor,
    sensor_factor,
    prior_scale,
    neighbours,
    edge_weight,
    noise,
):
    rank = sensor_factor.shape[0]
    block_len = sensor_factor.shape[1]
    all_slots = lax.all_gather(slot_factor, "day", axis=0, tiled=True)
    features = (day_factor[:, None, :] * all_slots[None, :, :]).reshape(-1, rank)
    row_total = features.shape[0] * lax.axis_size("day")
    outer_rows = (features[:, :, None] * features[:, None, :]).reshape(-1, rank * rank)
    mask_half = observed.astype(jnp.bfloat16)
    weighted = mask_half * y_obs
    dims = (((0,), (0,)), ((), ()))
    gram_sums = lax.dot_general(mask_half, outer_rows, dims, preferred_element_type=jnp.float32)
    right_sums = lax.dot_general(weighted, features, dims, preferred_element_type=jnp.float32)
    pieces = []
    for offset in (2, 1, 0, -1, -2):
        if offset == 0:
            pieces.append(sensor_factor)
        else:
            pieces.append(shifted(sensor_factor, "sensor", offset))
    window = jnp.concatenate(pieces, axis=1)
    base_col = (lax.axis_index("sensor") - 2) * block_len
    columns = neighbours - base_col
    picked = jnp.take(window, columns, axis=1).astype(jnp.float32)
    pulled = jnp.einsum("rns,ns->sr", picked, edge_weight)
    prior_diag = 1.0 + jnp.sum(edge_weight, axis=0)
    tau = 4.0 / row_total
    gram_part, right_part = (
        lax.psum_scatter(gram_sums, "day", scatter_dimension=0, tiled=True),
        lax.psum_scatter(right_sums, "day", scatter_dimension=0, tiled=True),
    )
    share_len = gram_part.shape[0]
    first_col = lax.axis_index("day") * share_len
    pulled_part = lax.dynamic_slice_in_dim(pulled, first_col, share_len, 0)
    diag_part = lax.dynamic_slice_in_dim(prior_diag, first_col, share_len, 0)
    noise_part = lax.dynamic_slice_in_dim(noise, first_col, share_len, 1)
    solved = solve_block(
        gram_part, right_part, pulled_part, diag_part, prior_scale, noise_part.T, tau
    )
    return lax.all_gather(solved.T, "day", axis=1, tiled=True)


def solution(mesh):
    return jax.shard_map(
        shards,
        mesh=mesh,
        in_specs=(
            P("day", "sensor"),
            P("day", "sensor"),
            P("day", None),
            P("day", None),
            P(None, "sensor"),
            P(),
            P(None, "sensor"),
            P(None, "sensor"),
            P(None, "sensor"),
        ),
        out_specs=P(None, "sensor"),
        check_vma=False,
    )
```

profile of v0, /device:TPU:0, one launch (start us, length us, event | category | flops | bytes accessed | tf_op | source)
XLA Modules:
  0.0 547.4 jit_solution(2110799887699905906)
XLA Ops:
  6.5 5.7 %all-gather = bf16[2,144,64]{1,2,0:T(8,128)(2,1)S(1)} all-gather(bf16[1,144,64]{1,2,0:T(8,128)(2,1)} %bitcast.69), channel_id=1, replica_groups=mesh['sensor'=16,'day'=2] {'day'}, dimensions={0}, use_global_device_ids=true | all-gather | bytes 55296 | tf_op jit(solution)/shard_map/all_gather | solution.py:45
  13.6 2.2 fusion.1
  15.9 5.5 broadcast_multiply_fusion
  21.4 6.4 %convolution_bitcast_fusion = f32[128,4096]{0,1:T(8,128)S(1)} fusion(bf16[1440,4096]{0,1:T(8,128)(2,1)} %bitcast.64, s32[1440,128]{1,0:T(8,128)S(1)} %copy-done.1), kind=kOutput, calls=%fused_computation.2 | convolution fusion | flops 1510133760 | bytes 14630912 | tf_op jit(solution)/shard_map/dot_general | solution.py:52
  27.8 1.9 copy.87
  30.6 3.9 collective-permute-start
  37.1 1.5 collective-permute-start.3
  39.0 1.7 collective-permute-done.2
  40.6 4.7 collective-permute-done.3
  45.4 1.9 gather_fusion
  48.7 14.8 %reduce-scatter.7.cloned.1.call-done = f32[64,4096]{1,0:T(8,128)} async-done(((f32[128,4096]{1,0:T(8,128)}), f32[64,4096]{1,0:T(8,128)}) %reduce-scatter.7.cloned.1.call-update) | async-done | bytes 1048592 | tf_op jit(solution)/shard_map/reduce_scatter | solution.py:68
  64.8 2.2 mul.97
  67.0 1.9 copy.63
  68.9 1.6 multiply_add_fusion
  70.5 2.9 copy.64
  73.4 3.3 fusion
  76.7 376.8 %custom-call.10 = f32[64,64,64]{2,1,0:T(8,128)} custom-call(f32[64,64,64]{2,1,0:T(8,128)} %fusion), custom_call_target="Cholesky" | custom-call | tf_op jit(solution)/shard_map/jit(cholesky)/cholesky | solution.py:19
  453.5 2.4 copy.65
  456.6 1.7 select_bitcast_fusion
  458.3 67.2 %custom-call.13 = f32[64,1,64,64]{0,2,3,1:T(8,128)S(1)} custom-call(f32[64,1,64,64]{0,3,2,1:T(8,128)} %select_bitcast_fusion), custom_call_target="InvertDiagBlocksLowerTriangular" | custom-call | tf_op jit(solution)/shard_map/triangular_solve/custom-call.2 | solution.py:23
  526.9 3.1 copy.79
  530.0 1.9 convolution_bitcast_fusion.1
  531.9 3.4 fusion.9
  535.3 4.6 all_gather.7
  (54 shorter events, 10.6 us)
Async XLA Ops:
  6.5 41.2 %reduce-scatter.5.cloned.1.call-start = ((), (), s32[]{:S(2)}) async-start(), calls=%async_computation.2 | async-start | bytes 98304 | tf_op jit(solution)/shard_map/reduce_scatter | solution.py:69
  15.9 5.5 %copy-start.1 = (s32[1440,128]{1,0:T(8,128)S(1)}, s32[1440,128]{1,0:T(8,128)}, u32[]{:S(2)}) copy-start(s32[1440,128]{1,0:T(8,128)} %param.12) | copy-start | bytes 2211844
  15.9 47.6 %reduce-scatter.7.cloned.1.call-start = ((), (), s32[]{:S(2)}) async-start(), calls=%async_computation.3 | async-start | bytes 3145728 | tf_op jit(solution)/shard_map/reduce_scatter | solution.py:68
  29.7 0.7 copy-start.3
  29.7 8.8 %copy-start.4 = (f32[6,128]{1,0:T(8,128)S(1)}, f32[6,128]{1,0:T(8,128)}, u32[]{:S(2)}) copy-start(f32[6,128]{1,0:T(8,128)} %param.18) | copy-start | bytes 9220
  29.7 8.9 %copy-start.5 = (s32[6,128]{1,0:T(8,128)S(1)}, s32[6,128]{1,0:T(8,128)}, u32[]{:S(2)}) copy-start(s32[6,128]{1,0:T(8,128)} %param.17) | copy-start | bytes 9220
  29.7 18.0 %copy-start.2 = (f32[64,128]{1,0:T(8,128)S(1)}, f32[64,128]{1,0:T(8,128)}, u32[]{:S(2)}) copy-start(f32[64,128]{1,0:T(8,128)} %param.19) | copy-start | bytes 98308
  29.7 18.0 %copy-start.6 = (f32[64]{0:T(128)S(1)}, f32[64]{0:T(128)}, u32[]{:S(2)}) copy-start(f32[64]{0:T(128)} %param.16) | copy-start | bytes 772
  30.6 8.4 %collective-permute-start = (bf16[64,128]{0,1:T(8,128)(2,1)S(1)}, bf16[64,128]{0,1:T(8,128)(2,1)S(1)}, u32[]{:S(2)}, u32[]{:S(2)}) collective-permute-start(bf16[64,128]{0,1:T(8,128)(2,1)S(1)} %copy.67), channel_id=1, source_target_pairs={{0,4},{2,6},{4,8},{6,10},{8,12},{10,14},{12,16},{14,18},{16,20},{1... | collective-permute-start | bytes 49160 | tf_op jit(solution)/shard_map/ppermute | solution.py:10
  34.5 4.5 collective-permute-start.1
  35.8 4.9 collective-permute-start.2
  37.1 8.3 %collective-permute-start.3 = (bf16[64,128]{0,1:T(8,128)(2,1)S(1)}, bf16[64,128]{0,1:T(8,128)(2,1)S(1)}, u32[]{:S(2)}, u32[]{:S(2)}) collective-permute-start(bf16[64,128]{0,1:T(8,128)(2,1)S(1)} %copy.67), channel_id=1, source_target_pairs={{4,0},{6,2},{8,4},{10,6},{12,8},{14,10},{16,12},{18,14},{20,16},{2... | collective-permute-start | bytes 49160 | tf_op jit(solution)/shard_map/ppermute | solution.py:10
  525.6 1.3 copy-start
Sparse Core Ops, SparseCore 0:
  16.0 11.6 reduce-scatter.4
  29.9 33.5 reduce-scatter.6
where the time goes:
time: 548 us; the launch traced here: 547 us
  other arithmetic  460 us (84%)
  waiting for transfers between devices  21.2 us (4%)
  local copies, waits for them, and re-layouts  20.3 us (4%)
  matrix products  14.2 us (3%)
  between operations  13.7 us (2%)
  blocking collectives  10.3 us (2%)
  starting transfers between devices  8.01 us (1%)
    another operation x4, other arithmetic, solve_block(): factor_low = jnp.linalg.cholesky(precision)  378 us
    another operation x3, other arithmetic, solve_block(): lax.linalg.triangular_solve(factor_low, halfway, left_side=True, lower=Tr...  69 us
    reduce_scatter x1, waiting for transfers between devices, shards(): lax.psum_scatter(gram_sums, 'day', scatter_dimension=0, tiled=True)  14.8 us
  transfers between devices with their start and end apart: 6, of which 3 were waited for; matrix products, arithmetic and copies ran while one was open for 3% of the time, Pallas kernels for 0%

commit v1 on v0

v1 whole, which is shorter than its diff:
```python
import jax
import jax.numpy as jnp
from jax import lax
from jax.experimental import pallas as pl
from jax.experimental.pallas import tpu as pltpu
from jax.sharding import PartitionSpec as P

RANK = 64
LANES = 128
HALF = 64
BLOCKS = RANK // 8


def lane_low(shape):
    return lax.broadcasted_iota(jnp.int32, shape, len(shape) - 1) < HALF


def both_halves(tile, upper):
    other = pltpu.roll(tile, HALF, 1)
    low = lane_low(tile.shape)
    return jnp.where(low, other, tile) if upper else jnp.where(low, tile, other)


def row_of(tile, index):
    return jnp.broadcast_to(tile[index : index + 1, :], tile.shape)


def factor_and_solve(load_columns, target, noise_tile, cols, wide, inv_diag, halfway, found):
    target = list(target)
    for block in range(BLOCKS):
        first = block // 2
        upper = block % 2 == 1
        count = 4 - first
        columns = load_columns(block)
        if block > 0:

            def subtract(k, carry):
                done = [cols[k, pl.ds(8 * q, 8), :] for q in range(first, 4)]
                out = []
                for c in range(8):
                    scale = jnp.broadcast_to(wide[k, pl.ds(8 * block + c, 1), :], (8, LANES))
                    out.extend(carry[c * count + q] - done[q] * scale for q in range(count))
                return tuple(out)

            flat = tuple(tile for column in columns for tile in column)
            flat = lax.fori_loop(0, 8 * block, subtract, flat, unroll=2)
            columns = [list(flat[c * count : (c + 1) * count]) for c in range(8)]
        corner = [both_halves(column[0], upper) for column in columns]
        side = both_halves(target[first], upper)
        for c in range(8):
            j = 8 * block + c
            inverse = lax.rsqrt(row_of(corner[c], c))
            corner[c] = corner[c] * inverse
            columns[c] = [tile * inverse for tile in columns[c]]
            solved = row_of(side, c) * inverse
            side = side - corner[c] * solved
            for q in range(count):
                target[first + q] = target[first + q] - columns[c][q] * solved
            for later in range(c + 1, 8):
                scale = row_of(corner[c], later)
                corner[later] = corner[later] - corner[c] * scale
                columns[later] = [
                    tile - own * scale for tile, own in zip(columns[later], columns[c])
                ]
            inv_diag[j] = inverse
            halfway[pl.ds(j, 1), :] = solved[0:1, :]
        for c in range(8):
            j = 8 * block + c
            for q in range(count):
                tile = columns[c][q]
                row = 16 * (first + q)
                cols[j, pl.ds(8 * (first + q), 8), :] = tile
                if row >= 8 * block:
                    wide[j, pl.ds(row, 8), :] = both_halves(tile, False)
                wide[j, pl.ds(row + 8, 8), :] = both_halves(tile, True)

    packed = [None] * 4
    low = lane_low((8, LANES))
    below = None
    for block in reversed(range(BLOCKS)):
        first = block // 2
        upper = block % 2 == 1
        right = halfway[pl.ds(8 * block, 8), :] + noise_tile(block)
        remain = []
        for c in range(8):
            j = 8 * block + c
            total = row_of(right, c)
            parts = None
            for q in range(first, 4):
                if q == first and upper:
                    continue
                if q == first:
                    term = jnp.where(low, 0.0, cols[j, pl.ds(8 * q, 8), :] * below)
                else:
                    term = cols[j, pl.ds(8 * q, 8), :] * packed[q]
                parts = term if parts is None else parts + term
            if parts is not None:
                sums = jnp.sum(parts, axis=0, keepdims=True)
                sums = jnp.broadcast_to(sums, (8, LANES))
                total = total - (sums + pltpu.roll(sums, HALF, 1))
            remain.append(total)
        values = [None] * 8
        for c in reversed(range(8)):
            values[c] = remain[c] * inv_diag[8 * block + c]
            for earlier in range(c):
                scale = jnp.broadcast_to(
                    wide[8 * block + earlier, pl.ds(8 * block + c, 1), :], (8, LANES)
                )
                remain[earlier] = remain[earlier] - scale * values[c]
        rows = lax.broadcasted_iota(jnp.int32, (8, LANES), 0)
        tile = values[0]
        for c in range(1, 8):
            tile = jnp.where(rows == c, values[c], tile)
        found[pl.ds(8 * block, 8), :] = tile
        if upper:
            below = tile
        else:
            packed[first] = jnp.where(low, tile, below)
            below = None
    return packed


def diagonal_tile(block, c, value):
    shape = (8, LANES)
    rows = lax.broadcasted_iota(jnp.int32, shape, 0)
    low = lane_low(shape)
    half = low if block % 2 == 0 else jnp.logical_not(low)
    return jnp.where((rows == c) & half, value, 0.0)


def solve_kernel(squares, target, noise, prior, out, cols, wide, inv_diag, halfway):
    def load_columns(block):
        first = block // 2
        own = prior[pl.ds(8 * block, 8), :]
        columns = []
        for c in range(8):
            j = 8 * block + c
            tiles = [squares[j, pl.ds(8 * q, 8), :] for q in range(first, 4)]
            tiles[0] = tiles[0] + diagonal_tile(block, c, own)
            columns.append(tiles)
        return columns

    targets = [target[pl.ds(8 * q, 8), :] for q in range(4)]
    factor_and_solve(
        load_columns,
        targets,
        lambda block: noise[pl.ds(8 * block, 8), :],
        cols,
        wide,
        inv_diag,
        halfway,
        out,
    )


def solver_scratch():
    return [
        pltpu.VMEM((RANK, 32, LANES), jnp.float32),
        pltpu.VMEM((RANK, RANK, LANES), jnp.float32),
        pltpu.VMEM((RANK, 8, LANES), jnp.float32),
        pltpu.VMEM((RANK, LANES), jnp.float32),
    ]


def pack_rows(rows):
    lead = rows.shape[:-2]
    split = rows.reshape(lead + (4, 2, 8, HALF))
    return jnp.swapaxes(split, -3, -2).reshape(lead + (32, LANES))


def solve_block(gram, right, pulled, prior_diag, prior_scale, noise, tau):
    share = right.shape[1]

    def fill(array, value=0.0):
        pad = [(0, 0)] * (array.ndim - 1) + [(0, HALF - share)]
        return jnp.pad(array, pad, constant_values=value)

    target = tau * right + prior_scale[:, None] * pulled
    prior = prior_scale[:, None] * fill(prior_diag, 1.0)[None, :]
    twice = lambda array: jnp.concatenate([array, array], axis=1)
    spec = pl.BlockSpec(memory_space=pltpu.VMEM)
    solved = pl.pallas_call(
        solve_kernel,
        out_shape=jax.ShapeDtypeStruct((RANK, LANES), jnp.float32),
        in_specs=[spec] * 4,
        out_specs=spec,
        scratch_shapes=solver_scratch(),
        compiler_params=pltpu.CompilerParams(vmem_limit_bytes=24 * 1024 * 1024),
        name="solve_sensors",
    )(tau * pack_rows(fill(gram)), pack_rows(fill(target)), twice(fill(noise)), twice(prior))
    return solved[:, :share]


def shifted(shard, axis, by):
    size = lax.axis_size(axis)
    pairs = [(i, i + by) for i in range(size) if 0 <= i + by < size]
    return lax.ppermute(shard, axis, pairs)


def general_shards(
    y_obs,
    observed,
    day_factor,
    slot_factor,
    sensor_factor,
    prior_scale,
    neighbours,
    edge_weight,
    noise,
):
    rank = sensor_factor.shape[0]
    block_len = sensor_factor.shape[1]
    all_slots = lax.all_gather(slot_factor, "day", axis=0, tiled=True)
    features = (day_factor[:, None, :] * all_slots[None, :, :]).reshape(-1, rank)
    row_total = features.shape[0] * lax.axis_size("day")
    outer_rows = (features[:, :, None] * features[:, None, :]).reshape(-1, rank * rank)
    mask_half = observed.astype(jnp.bfloat16)
    weighted = mask_half * y_obs
    dims = (((0,), (0,)), ((), ()))
    gram_sums = lax.dot_general(outer_rows, mask_half, dims, preferred_element_type=jnp.float32)
    right_sums = lax.dot_general(features, weighted, dims, preferred_element_type=jnp.float32)
    pieces = []
    for offset in (2, 1, 0, -1, -2):
        if offset == 0:
            pieces.append(sensor_factor)
        else:
            pieces.append(shifted(sensor_factor, "sensor", offset))
    window = jnp.concatenate(pieces, axis=1)
    base_col = (lax.axis_index("sensor") - 2) * block_len
    columns = neighbours - base_col
    picked = jnp.take(window, columns, axis=1).astype(jnp.float32)
    pulled = jnp.einsum("rns,ns->rs", picked, edge_weight)
    prior_diag = 1.0 + jnp.sum(edge_weight, axis=0)
    tau = 4.0 / row_total
    sums = jnp.concatenate([gram_sums, right_sums], axis=0)
    sums = lax.psum_scatter(sums, "day", scatter_dimension=1, tiled=True)
    share_len = sums.shape[1]
    first_col = lax.axis_index("day") * share_len
    part = lambda array: lax.dynamic_slice_in_dim(array, first_col, share_len, array.ndim - 1)
    solved = solve_block(
        sums[: rank * rank].reshape(rank, rank, share_len),
        sums[rank * rank :],
        part(pulled),
        part(prior_diag),
        prior_scale,
        part(noise),
        tau,
    )
    return lax.all_gather(solved, "day", axis=1, tiled=True)


def solution(mesh):
    return jax.shard_map(
        general_shards,
        mesh=mesh,
        in_specs=(
            P("day", "sensor"),
            P("day", "sensor"),
            P("day", None),
            P("day", None),
            P(None, "sensor"),
            P(),
            P(None, "sensor"),
            P(None, "sensor"),
            P(None, "sensor"),
        ),
        out_specs=P(None, "sensor"),
        check_vma=False,
    )
```

time: 548 us -> 85.3 us (0.16)
  other arithmetic: 460 us -> 6.37 us
  local copies, waits for them, and re-layouts: 20.3 us -> 12.5 us
  matrix products: 14.2 us -> 6.63 us
    another operation x7 -> x0, other arithmetic: 447 us -> none  [the longest x4 378 us: solve_block(): factor_low = jnp.linalg.cholesky(precision)]
    unnamed x2, waiting for transfers between devices: 0.03 us -> 16.6 us
    reduce_scatter x2 -> x0, waiting for transfers between devices: 14.8 us -> none  [the longest x1 14.8 us: shards(): lax.psum_scatter(gram_sums, 'day', scatter_dimension=0, tiled=True)]
    another operation x3 -> x0, local copies, waits for them, and re-layouts: 5.53 us -> none  [the longest x1 3.1 us: solve_block(): lax.linalg.triangular_solve(factor_low, target[:, :, None], left_side=Tru...]
  transfers between devices with their start and end apart: 6 -> 5, of which waited for: 3 -> 3; matrix products, arithmetic and copies ran while one was open for 3% -> 3% of each run, Pallas kernels for 0% -> 0%
where the time goes in v1:
time: 85.3 us; the launch traced here: 84.8 us
  waiting for transfers between devices  23.3 us (27%)
  between operations  13.7 us (16%)
  local copies, waits for them, and re-layouts  12.5 us (15%)
  blocking collectives  10.5 us (12%)
  starting transfers between devices  7.79 us (9%)
  matrix products  6.63 us (8%)
  other arithmetic  6.37 us (7%)
  Pallas kernels  4.13 us (5%)
    unnamed x2, waiting for transfers between devices  16.6 us
    ppermute x4, starting transfers between devices, shifted(): return lax.ppermute(shard, axis, pairs)  7.79 us
    ppermute x4, waiting for transfers between devices, shifted(): return lax.ppermute(shard, axis, pairs)  6.7 us
    dot_general x1, matrix products, general_shards(): lax.dot_general(outer_rows, mask_half, dims, preferred_element_type=jnp.f...  6.43 us
    all_gather x1, blocking collectives, general_shards(): all_slots = lax.all_gather(slot_factor, 'day', axis=0, tiled=True)  5.88 us
    mul x1, other arithmetic, general_shards(): features[:, :, None] * features[:, None, :]  5.43 us
    unnamed x25, local copies, waits for them, and re-layouts  4.76 us
    all_gather x1, blocking collectives, general_shards(): return lax.all_gather(solved, 'day', axis=1, tiled=True)  4.59 us
  transfers between devices with their start and end apart: 5, of which 3 were waited for; matrix products, arithmetic and copies ran while one was open for 3% of the time, Pallas kernels for 0%

profile of v1, /device:TPU:0, one launch (start us, length us, event | category | flops | bytes accessed | tf_op | source)
XLA Modules:
  0.0 84.8 jit_solution(4297392589101729784)
XLA Ops:
  6.5 5.9 %all-gather = bf16[2,144,64]{1,2,0:T(8,128)(2,1)S(1)} all-gather(bf16[1,144,64]{1,2,0:T(8,128)(2,1)} %bitcast.39), channel_id=1, replica_groups=mesh['sensor'=16,'day'=2] {'day'}, dimensions={0}, use_global_device_ids=true | all-gather | bytes 55296 | tf_op jit(solution)/shard_map/all_gather | solution.py:213
  12.6 0.8 copy.35
  13.5 0.2 mul.96
  13.8 5.4 %broadcast_multiply_fusion = bf16[1440,64,64]{0,2,1:T(8,128)(2,1)} fusion(bf16[1440,64]{0,1:T(8,128)(2,1)S(1)} %mul.96), kind=kLoop, calls=%fused_computation.1 | loop fusion | flops 5898240 | bytes 11980800 | tf_op jit(solution)/shard_map/mul | solution.py:216
  19.4 6.4 %fusion.3 = f32[4096,128]{1,0:T(8,128)S(1)} fusion(bf16[1440,4096]{0,1:T(8,128)(2,1)} %bitcast.30, s32[1440,128]{1,0:T(8,128)S(1)} %copy-done.1), kind=kOutput, calls=%fused_computation.10 | convolution fusion | flops 1510133760 | bytes 14630912 | tf_op jit(solution)/shard_map/dot_general | solution.py:220
  26.0 2.3 %copy.53 = f32[4160,128]{0,1:T(8,128)} copy(f32[4160,128]{1,0:T(8,128)S(1)} %pad_maximum_fusion) | data formatting | bytes 4259840
  28.3 0.7 copy-done.4
  29.1 3.9 %collective-permute-start = (bf16[64,128]{0,1:T(8,128)(2,1)S(1)}, bf16[64,128]{0,1:T(8,128)(2,1)S(1)}, u32[]{:S(2)}, u32[]{:S(2)}) collective-permute-start(bf16[64,128]{0,1:T(8,128)(2,1)S(1)} %copy.38), channel_id=1, source_target_pairs={{0,4},{2,6},{4,8},{6,10},{8,12},{10,14},{12,16},{14,18},{16,20},{1... | collective-permute-start | bytes 49160 | tf_op jit(solution)/shard_map/ppermute | solution.py:197
  33.0 1.3 %collective-permute-start.1 = (bf16[64,128]{0,1:T(8,128)(2,1)S(1)}, bf16[64,128]{0,1:T(8,128)(2,1)S(1)}, u32[]{:S(2)}, u32[]{:S(2)}) collective-permute-start(bf16[64,128]{0,1:T(8,128)(2,1)S(1)} %copy.38), channel_id=1, source_target_pairs={{0,2},{2,4},{4,6},{6,8},{8,10},{10,12},{12,14},{14,16},{16,18},{18... | collective-permute-start | bytes 49160 | tf_op jit(solution)/shard_map/ppermute | solution.py:197
  34.3 1.3 %collective-permute-start.2 = (bf16[64,128]{0,1:T(8,128)(2,1)S(1)}, bf16[64,128]{0,1:T(8,128)(2,1)S(1)}, u32[]{:S(2)}, u32[]{:S(2)}) collective-permute-start(bf16[64,128]{0,1:T(8,128)(2,1)S(1)} %copy.38), channel_id=1, source_target_pairs={{2,0},{4,2},{6,4},{8,6},{10,8},{12,10},{14,12},{16,14},{18,16},{20... | collective-permute-start | bytes 49160 | tf_op jit(solution)/shard_map/ppermute | solution.py:197
  35.6 1.3 %collective-permute-start.3 = (bf16[64,128]{0,1:T(8,128)(2,1)S(1)}, bf16[64,128]{0,1:T(8,128)(2,1)S(1)}, u32[]{:S(2)}, u32[]{:S(2)}) collective-permute-start(bf16[64,128]{0,1:T(8,128)(2,1)S(1)} %copy.38), channel_id=1, source_target_pairs={{4,0},{6,2},{8,4},{10,6},{12,8},{14,10},{16,12},{18,14},{20,16},{2... | collective-permute-start | bytes 49160 | tf_op jit(solution)/shard_map/ppermute | solution.py:197
  37.2 2.0 %collective-permute-done.2 = bf16[64,128]{0,1:T(8,128)(2,1)S(1)} collective-permute-done((bf16[64,128]{0,1:T(8,128)(2,1)S(1)}, bf16[64,128]{0,1:T(8,128)(2,1)S(1)}, u32[]{:S(2)}, u32[]{:S(2)}) %collective-permute-start.2) | collective-permute-done | bytes 16416 | tf_op jit(solution)/shard_map/ppermute | solution.py:197
  39.2 4.7 %collective-permute-done.3 = bf16[64,128]{0,1:T(8,128)(2,1)S(1)} collective-permute-done((bf16[64,128]{0,1:T(8,128)(2,1)S(1)}, bf16[64,128]{0,1:T(8,128)(2,1)S(1)}, u32[]{:S(2)}, u32[]{:S(2)}) %collective-permute-start.3) | collective-permute-done | bytes 16416 | tf_op jit(solution)/shard_map/ppermute | solution.py:197
  44.0 1.9 %gather_fusion = bf16[768,64]{1,0:T(8,128)(2,1)S(1)} fusion(bf16[64,640]{0,1:T(8,128)(2,1)S(1)} %constant_dynamic-update-slice_fusion, s32[1024]{0:T(1024)S(1)} %pad_clamp_fusion), kind=kCustom, calls=%fused_computation | custom fusion | bytes 199680 | tf_op jit(solution)/shard_map/jit(_take)/gather | solution.py:231
  45.8 0.3 multiply_reduce_fusion
  46.2 16.6 %reduce-scatter.4.cloned.1.call-done = f32[64,4160]{1,0:T(8,128)} async-done(((f32[128,4160]{1,0:T(8,128)}), f32[64,4160]{1,0:T(8,128)}) %reduce-scatter.4.cloned.1.call-update) | async-done | bytes 1064976
  62.8 1.3 %slice.14 = f32[4096,64]{0,1:T(8,128)S(1)} slice(f32[4160,64]{0,1:T(8,128)} %bitcast.34), slice={[0:4096], [0:64]} | slice | bytes 2097152 | tf_op jit(solution)/shard_map/slice | solution.py:241
  64.1 0.8 slice.15
  64.8 0.6 copy.55
  65.6 1.3 %copy.60 = f32[64,4,2,8,64]{4,2,3,1,0:T(2,128)S(1)} copy(f32[64,4,2,8,64]{4,3,2,1,0:T(8,128)S(1)} %bitcast.32) | data formatting | bytes 2097152 | tf_op jit(solution)/shard_map/mul | solution.py:190
  66.9 1.1 %mul.106.squares = f32[64,32,128]{2,1,0:T(8,128)S(1)} reshape(f32[64,4,8,2,64]{4,3,2,1,0:T(2,128)S(1)} %bitcast.33) | data formatting | bytes 2097152 | tf_op jit(solution)/shard_map/mul | solution.py:190
  68.5 4.1 %solve_sensors.1 = f32[64,128]{1,0:T(8,128)S(1)} custom-call(f32[64,32,128]{2,1,0:T(8,128)S(1)} %mul.106.squares, f32[32,128]{1,0:T(8,128)S(1)} %reshape.58.target, f32[64,128]{1,0:T(8,128)S(1)} %get-tuple-element.7.noise, f32[64,128]{1,0:T(8,128)S(1)} %get-tuple-element.8.prior), custom_call_target="tpu_custom_call" | custom-call | tf_op jit(solution)/shard_map/solve_sensors/pallas_call | solution.py:182
  72.7 4.6 %all_gather.7 = f32[64,128]{0,1:T(8,128)S(1)} all-gather(f32[64,64]{0,1:T(8,128)S(1)} %copy.44), channel_id=1, replica_groups=mesh['sensor'=16,'day'=2] {'day'}, dimensions={1}, use_global_device_ids=true | all-gather | bytes 49152 | tf_op jit(solution)/shard_map/all_gather | solution.py:249
  77.3 0.7 copy.45
  (44 shorter events, 1.8 us)
Async XLA Ops:
  6.5 30.4 %copy-start = (f32[64,128]{1,0:T(8,128)S(1)}, f32[64,128]{1,0:T(8,128)}, u32[]{:S(2)}) copy-start(f32[64,128]{1,0:T(8,128)} %param.17) | copy-start | bytes 98308
  6.5 56.2 %reduce-scatter.4.cloned.1.call-start = ((), (), s32[]{:S(2)}) async-start(), calls=%async_computation.1 | async-start | bytes 3244032
  13.8 5.5 %copy-start.1 = (s32[1440,128]{1,0:T(8,128)S(1)}, s32[1440,128]{1,0:T(8,128)}, u32[]{:S(2)}) copy-start(s32[1440,128]{1,0:T(8,128)} %param.10) | copy-start | bytes 2211844
  13.8 5.4 %copy-start.2 = (bf16[1440,128]{1,0:T(8,128)(2,1)S(1)}, bf16[1440,128]{1,0:T(8,128)(2,1)}, u32[]{:S(2)}) copy-start(bf16[1440,128]{1,0:T(8,128)(2,1)} %param.9) | copy-start | bytes 1105924
  28.3 0.7 copy-start.4
  28.3 8.7 %copy-start.3 = (f32[6,128]{1,0:T(8,128)S(1)}, f32[6,128]{1,0:T(8,128)}, u32[]{:S(2)}) copy-start(f32[6,128]{1,0:T(8,128)} %param.16) | copy-start | bytes 9220
  28.3 8.8 %copy-start.5 = (s32[6,128]{1,0:T(8,128)S(1)}, s32[6,128]{1,0:T(8,128)}, u32[]{:S(2)}) copy-start(s32[6,128]{1,0:T(8,128)} %param.15) | copy-start | bytes 9220
  29.1 8.1 %collective-permute-start = (bf16[64,128]{0,1:T(8,128)(2,1)S(1)}, bf16[64,128]{0,1:T(8,128)(2,1)S(1)}, u32[]{:S(2)}, u32[]{:S(2)}) collective-permute-start(bf16[64,128]{0,1:T(8,128)(2,1)S(1)} %copy.38), channel_id=1, source_target_pairs={{0,4},{2,6},{4,8},{6,10},{8,12},{10,14},{12,16},{14,18},{16,20},{1... | collective-permute-start | bytes 49160 | tf_op jit(solution)/shard_map/ppermute | solution.py:197
  33.0 4.2 %collective-permute-start.1 = (bf16[64,128]{0,1:T(8,128)(2,1)S(1)}, bf16[64,128]{0,1:T(8,128)(2,1)S(1)}, u32[]{:S(2)}, u32[]{:S(2)}) collective-permute-start(bf16[64,128]{0,1:T(8,128)(2,1)S(1)} %copy.38), channel_id=1, source_target_pairs={{0,2},{2,4},{4,6},{6,8},{8,10},{10,12},{12,14},{14,16},{16,18},{18... | collective-permute-start | bytes 49160 | tf_op jit(solution)/shard_map/ppermute | solution.py:197
  34.3 4.9 %collective-permute-start.2 = (bf16[64,128]{0,1:T(8,128)(2,1)S(1)}, bf16[64,128]{0,1:T(8,128)(2,1)S(1)}, u32[]{:S(2)}, u32[]{:S(2)}) collective-permute-start(bf16[64,128]{0,1:T(8,128)(2,1)S(1)} %copy.38), channel_id=1, source_target_pairs={{2,0},{4,2},{6,4},{8,6},{10,8},{12,10},{14,12},{16,14},{18,16},{20... | collective-permute-start | bytes 49160 | tf_op jit(solution)/shard_map/ppermute | solution.py:197
  35.6 8.3 %collective-permute-start.3 = (bf16[64,128]{0,1:T(8,128)(2,1)S(1)}, bf16[64,128]{0,1:T(8,128)(2,1)S(1)}, u32[]{:S(2)}, u32[]{:S(2)}) collective-permute-start(bf16[64,128]{0,1:T(8,128)(2,1)S(1)} %copy.38), channel_id=1, source_target_pairs={{4,0},{6,2},{8,4},{10,6},{12,8},{14,10},{16,12},{18,14},{20,16},{2... | collective-permute-start | bytes 49160 | tf_op jit(solution)/shard_map/ppermute | solution.py:197
  66.9 1.2 %copy-start.6 = (f32[64]{0:T(128)S(1)}, f32[64]{0:T(128)}, u32[]{:S(2)}) copy-start(f32[64]{0:T(128)} %param.14) | copy-start | bytes 772
Sparse Core Ops, SparseCore 0:
  28.4 34.2 reduce-scatter.3
